TPU v7x, 256 devices: a whole 4x4x8 slice. The times are simulated.
256 devices in a mesh: dp: 32 (over x_lo, z, core), slab: 8 (over y, x_hi).
Axes of the slice: x: 4 (x_hi: 2, x_lo: 2; x = x_hi * 2 + x_lo), y: 4, z: 8, core: 2. Of those that a mesh axis runs over, the one named last changes fastest.
Arguments:
- inputs: bfloat16 [32, 48, 36, 2048], P('dp', 'slab'), may hold values from -6 to 6
- weight: bfloat16 [3, 3, 2048, 256], replicated, may hold values from -0.046875 to 0.046875
- pre_norm: bfloat16 [32, 48, 36, 256], P('dp', 'slab'), may hold values from -50 to 50
- grad_norm: bfloat16 [32, 48, 36, 256], P('dp', 'slab'), may hold values from -6 to 6
- norm_gain: float32 [256], replicated, may hold values from 0.5 to 1.5
Outputs:
- input_grad: bfloat16 [32, 48, 36, 2048], P('dp', 'slab')
- weight_grad: float32 [3, 3, 2048, 256], P(None, None, ('dp', 'slab'))
- gain_grad: float32 [256], replicated
- bias_grad: float32 [256], replicated
All inputs are finite; a program needn't handle non-finite values.
Results may differ from a plain program's by a relative error of at most 0.0049.
Values may be sent and summed in bfloat16 or wider, within the bound.
A program may use at most 128 MiB of HBM per device.

v0:
```python
import jax
import jax.numpy as jnp
from jax import lax
from jax.sharding import PartitionSpec as P

DILATION_STEP = 24


EPSILON = 1e-05


def from_behind(block, axis, distance):
    devices = range(lax.axis_size(axis))
    route = [(i - distance, i) for i in devices if i - distance in devices]
    return lax.ppermute(block, axis, route)


def displace_columns(tensor_values, tap_displacement):
    padded_input = jnp.pad(tensor_values, ((0, 0), (DILATION_STEP, DILATION_STEP), (0, 0)))
    return padded_input[
        :,
        DILATION_STEP
        + tap_displacement : DILATION_STEP
        + tap_displacement
        + tensor_values.shape[1],
    ]


def per_device(inputs, weight, pre_norm, grad_norm, norm_gain):
    height_per_device = inputs.shape[1]
    width_dev = inputs.shape[2]
    channels_in = inputs.shape[3]
    channels_out = pre_norm.shape[3]
    cells = height_per_device * width_dev
    cell_count = cells * lax.axis_size("slab")
    slab_neighbour_steps = DILATION_STEP // height_per_device
    saved_f = pre_norm[0].astype(jnp.float32)
    running = lax.psum(jnp.sum(saved_f, axis=(0, 1)), "slab")
    mean_val = running / cell_count
    centred = saved_f - mean_val
    spread = lax.psum(jnp.sum(centred * centred, axis=(0, 1)), "slab")
    variance = spread / cell_count
    inv_std = lax.rsqrt(variance + EPSILON)
    zhat = centred * inv_std
    upstream_f = grad_norm[0].astype(jnp.float32)
    sum_g, sum_gz = lax.psum(
        (jnp.sum(upstream_f, axis=(0, 1)), jnp.sum(upstream_f * zhat, axis=(0, 1))), "slab"
    )
    gradient_before_norm = (
        norm_gain * inv_std * (upstream_f - sum_g / cell_count - zhat * (sum_gz / cell_count))
    ).astype(jnp.bfloat16)
    gain_grad, bias_grad = lax.psum((sum_gz, sum_g), "dp")
    grad_higher = from_behind(gradient_before_norm, "slab", slab_neighbour_steps)
    grad_lower = from_behind(gradient_before_norm, "slab", -slab_neighbour_steps)
    grad_sources = (grad_lower, gradient_before_norm, grad_higher)
    flat_grad = gradient_before_norm.reshape(cells, channels_out)
    input_higher = from_behind(inputs, "slab", slab_neighbour_steps)
    input_lower = from_behind(inputs, "slab", -slab_neighbour_steps)
    input_neighbours = (input_higher[0], inputs[0], input_lower[0])
    grad_in = jnp.zeros((cells, channels_in), jnp.float32)
    grads = []
    for row_kernel_tap in range(3):
        sender_slab = grad_sources[row_kernel_tap]
        stacked = jnp.stack(
            [
                displace_columns(sender_slab, -(column_kernel_tap - 1) * DILATION_STEP)
                for column_kernel_tap in range(3)
            ],
            axis=2,
        )
        stacked = stacked.reshape(cells, 3, channels_out)
        grad_in = grad_in + jnp.einsum(
            "pjo,jco->pc", stacked, weight[row_kernel_tap], preferred_element_type=jnp.float32
        )
        moved_in = jnp.stack(
            [
                displace_columns(
                    input_neighbours[row_kernel_tap], (column_kernel_tap - 1) * DILATION_STEP
                )
                for column_kernel_tap in range(3)
            ],
            axis=2,
        )
        moved_in = moved_in.reshape(cells, 3, channels_in)
        grads.append(
            jnp.einsum("pjc,po->jco", moved_in, flat_grad, preferred_element_type=jnp.float32)
        )
    local_grad = jnp.stack(grads)
    weight_grad = lax.psum_scatter(local_grad, ("dp", "slab"), scatter_dimension=2, tiled=True)
    input_grad = grad_in.astype(jnp.bfloat16).reshape(1, height_per_device, width_dev, channels_in)
    return (input_grad, weight_grad, gain_grad, bias_grad)


def solution(mesh):
    placed = (
        P("dp", "slab", None, None),
        P(),
        P("dp", "slab", None, None),
        P("dp", "slab", None, None),
        P(),
    )
    return jax.shard_map(
        per_device,
        mesh=mesh,
        in_specs=placed,
        out_specs=(P("dp", "slab", None, None), P(None, None, ("dp", "slab"), None), P(), P()),
        check_vma=False,
    )
```

profile of v0, /device:TPU:130, one launch (start us, length us, event | category | flops | bytes accessed | tf_op | source)
XLA Modules:
  0.0 1447.6 jit_solution(4080371177750066452)
XLA Ops:
  7.2 0.0 copy-start.2
  7.2 0.0 copy-start
  7.2 0.0 copy-start.1
  7.2 0.0 reduce-scatter.2.cloned.1.call-start
  7.2 1.4 collective-permute-start.3
  8.7 6.2 collective-permute-start.2
  14.9 0.9 convert_reduce_fusion
  15.8 21.3 %psum.42 = f32[256]{0:T(256)S(1)} all-reduce(f32[256]{0:T(256)S(1)} %convert_reduce_fusion), channel_id=1, replica_groups=mesh['dp'=32,'slab'=8] {'slab'}, use_global_device_ids=true, to_apply=%region_1.0 | all-reduce | flops 256 | bytes 2048 | tf_op jit(solution)/shard_map/psum | solution.py:38
  37.2 1.0 multiply_reduce_fusion
  38.1 20.4 %psum.43 = f32[256]{0:T(256)S(1)} all-reduce(f32[256]{0:T(256)S(1)} %multiply_reduce_fusion), channel_id=1, replica_groups=mesh['dp'=32,'slab'=8] {'slab'}, use_global_device_ids=true, to_apply=%region_3.0 | all-reduce | flops 256 | bytes 2048 | tf_op jit(solution)/shard_map/psum | solution.py:41
  58.5 0.9 convert_reduce_fusion.1
  59.5 0.7 fusion.77
  60.1 1.0 fusion.66
  61.2 2.6 fusion.44
  63.8 21.2 %all-reduce.7 = (f32[256]{0:T(256)S(1)}, f32[256]{0:T(256)S(1)}) all-reduce(f32[256]{0:T(256)S(1)} %fusion.66, f32[256]{0:T(256)S(1)} %convert_reduce_fusion.1), channel_id=1, replica_groups=mesh['dp'=32,'slab'=8] {'slab'}, use_global_device_ids=true, to_apply=%region_7.0 | all-reduce | flops 512 | bytes 4096 | tf_op jit(solution)/shard_map/psum | solution.py:46
  85.0 0.1 fusion.65
  85.1 2.6 convolution_bitcast_fusion.1
  87.7 0.2 fusion.46
  88.0 0.2 fusion.42
  88.2 1.4 convolution_bitcast_fusion
  89.6 1.4 convolution_bitcast_fusion.2
  91.0 6.7 pad_maximum_fusion
  97.6 0.0 reduce-scatter.2.cloned.1.call-update
  97.6 1.3 collective-permute-start
  98.9 6.1 collective-permute-start.1
  105.2 0.1 multiply_convert_fusion
  105.2 3.0 fusion.27
  108.2 48.0 %all-reduce.6 = (f32[256]{0:T(256)}, f32[256]{0:T(256)}) all-reduce(f32[256]{0:T(256)S(1)} %get-tuple-element.6, f32[256]{0:T(256)S(1)} %get-tuple-element.7), channel_id=1, replica_groups=mesh['dp'=32,'slab'=8] {'dp'}, use_global_device_ids=true, to_apply=%region_9.0 | all-reduce | flops 512 | bytes 4096 | tf_op jit(solution)/shard_map/psum | solution.py:52
  156.5 3.0 fusion.36
  159.5 3.0 fusion.39
  162.6 1.1 reshape.152
  163.7 1277.1 %reduce-scatter.2.cloned.1.call-done = f32[3,3,8,256]{3,2,1,0:T(8,128)} async-done(((f32[3,3,2048,256]{3,2,1,0:T(8,128)}), f32[3,3,8,256]{3,2,1,0:T(8,128)}) %reduce-scatter.2.cloned.1.call-update) | async-done | bytes 73744 | tf_op jit(solution)/shard_map/reduce_scatter | solution.py:89
  (22 shorter events, 0.3 us)
Async XLA Ops:
  7.2 77.9 %copy-start.2 = (bf16[1,6,36,2048]{3,2,1,0:T(8,128)(2,1)S(1)}, bf16[1,6,36,2048]{3,2,1,0:T(8,128)(2,1)}, u32[]{:S(2)}) copy-start(bf16[1,6,36,2048]{3,2,1,0:T(8,128)(2,1)} %param.5) | copy-start | bytes 2654212
  7.2 77.8 %copy-start = (bf16[1,6,36,256]{3,2,1,0:T(8,128)(2,1)S(1)}, bf16[1,6,36,256]{3,2,1,0:T(8,128)(2,1)}, u32[]{:S(2)}) copy-start(bf16[1,6,36,256]{3,2,1,0:T(8,128)(2,1)} %param.7) | copy-start | bytes 331780
  7.2 77.8 %copy-start.1 = (bf16[1,6,36,256]{3,2,1,0:T(8,128)(2,1)S(1)}, bf16[1,6,36,256]{3,2,1,0:T(8,128)(2,1)}, u32[]{:S(2)}) copy-start(bf16[1,6,36,256]{3,2,1,0:T(8,128)(2,1)} %param.8) | copy-start | bytes 331780
  7.2 1433.6 %reduce-scatter.2.cloned.1.call-start = ((), (), s32[]{:S(2)}) async-start(), calls=%async_computation.1 | async-start | bytes 18948096 | tf_op jit(solution)/shard_map/reduce_scatter | solution.py:89
  7.2 80.5 %collective-permute-start.3 = (bf16[1,6,36,2048]{3,2,1,0:T(8,128)(2,1)}, bf16[1,6,36,2048]{3,2,1,0:T(8,128)(2,1)S(1)}, u32[]{:S(2)}, u32[]{:S(2)}) collective-permute-start(bf16[1,6,36,2048]{3,2,1,0:T(8,128)(2,1)} %param.5), channel_id=1, source_target_pairs={{4,0},{5,1},{6,2},{7,3},{12,8},{13,9},{14,10},{15,11},{20,16},{21,... | collective-permute-start | bytes 2654216 | tf_op jit(solution)/shard_map/ppermute | solution.py:15
  8.7 79.3 %collective-permute-start.2 = (bf16[1,6,36,2048]{3,2,1,0:T(8,128)(2,1)}, bf16[1,6,36,2048]{3,2,1,0:T(8,128)(2,1)S(1)}, u32[]{:S(2)}, u32[]{:S(2)}) collective-permute-start(bf16[1,6,36,2048]{3,2,1,0:T(8,128)(2,1)} %param.5), channel_id=1, source_target_pairs={{0,4},{1,5},{2,6},{3,7},{8,12},{9,13},{10,14},{11,15},{16,20},{17,... | collective-permute-start | bytes 2654216 | tf_op jit(solution)/shard_map/ppermute | solution.py:15
  97.6 58.6 %collective-permute-start = (bf16[6,36,256]{2,1,0:T(8,128)(2,1)S(1)}, bf16[6,36,256]{2,1,0:T(8,128)(2,1)S(1)}, u32[]{:S(2)}, u32[]{:S(2)}) collective-permute-start(bf16[6,36,256]{2,1,0:T(8,128)(2,1)S(1)} %fusion.65), channel_id=1, source_target_pairs={{4,0},{5,1},{6,2},{7,3},{12,8},{13,9},{14,10},{15,11},{20,16},{21,... | collective-permute-start | bytes 331784 | tf_op jit(solution)/shard_map/ppermute | solution.py:15
  98.9 57.4 %collective-permute-start.1 = (bf16[6,36,256]{2,1,0:T(8,128)(2,1)S(1)}, bf16[6,36,256]{2,1,0:T(8,128)(2,1)S(1)}, u32[]{:S(2)}, u32[]{:S(2)}) collective-permute-start(bf16[6,36,256]{2,1,0:T(8,128)(2,1)S(1)} %fusion.65), channel_id=1, source_target_pairs={{0,4},{1,5},{2,6},{3,7},{8,12},{9,13},{10,14},{11,15},{16,20},{17,... | collective-permute-start | bytes 331784 | tf_op jit(solution)/shard_map/ppermute | solution.py:15
Sparse Core Ops, SparseCore 0:
  97.8 1342.9 reduce-scatter.1
where the time goes:
time: 1450 us
  waiting for transfers between devices  1280 us (88%)
  blocking collectives  111 us (8%)
  starting transfers between devices  15 us (1%)
    reduce_scatter x1, waiting for transfers between devices, per_device(): lax.psum_scatter(local_grad, ('dp', 'slab'), scatter_dimension=2, tiled=T...  1280 us
    psum x1, blocking collectives, per_device(): gain_grad, bias_grad = lax.psum((sum_gz, sum_g), 'dp')  48 us
  transfers between devices with their start and end apart: 5, of which 1 were waited for; matrix products, arithmetic and copies ran while one was open for 1% of the time, Pallas kernels for 0%

commit v1 on v0

v1 whole, which is shorter than its diff:
```python
import functools

import jax
import jax.numpy as jnp
from jax import lax
from jax.experimental import pallas as pl
from jax.experimental.pallas import tpu as pltpu
from jax.sharding import PartitionSpec as P

MESH = pl.DeviceIdType.MESH
F32 = jnp.float32
BF16 = jnp.bfloat16
EPSILON = 1e-05
TAPS = ((1, 1), (0, 1), (2, 1), (1, 0), (1, 2), (0, 0), (0, 2), (2, 0), (2, 2))


def kernel(
    sizes,
    x_hbm, w_hbm, pre_hbm, gn_hbm, gain_ref,
    gin_ref, wg_ref, gg_ref, bg_ref,
    pre_v, gn_v, st, xr, gr, xf, xc, gf, gc, wv, gin_v,
    dw, crecv, keep, xsend, xrecv, fsend, frecv,
    gb, gbc, gbk, gbx, gbs, gbf,
    load_sem, w_sem, x_loc, gin_sem, f_loc, gb_loc,
    st_s, st_r, x_s, x_r, g_s, g_r, c_s, c_r, l_s, l_r, f_s, f_r,
    gc_s, gc_r, gl_s, gl_r, gf_s, gf_r,
):
    ns, nz, rows, cols, cin, cout = sizes
    gran = cin // (2 * ns)
    pad = xf.shape[1]
    side = xc.shape[1]
    third = cols // 3
    cells = rows * cols * ns
    slab = lax.axis_index("slab")
    dp = lax.axis_index("dp")
    core = lax.rem(dp, 2)
    z = lax.rem(lax.div(dp, 2), nz)
    xlo = lax.div(dp, 2 * nz)
    other_core = {"dp": dp + 1 - 2 * core, "slab": slab}
    other_x = {"dp": dp + (1 - 2 * xlo) * (2 * nz), "slab": slab}
    own_final = z == slab

    def peer(q):
        return lax.rem(slab + q, ns)

    def source(q):
        return lax.rem(slab + ns - q, ns)

    def image_device(s):
        return {"dp": dp, "slab": s}

    def owner(q):
        return {"dp": (xlo * nz + slab) * 2 + core, "slab": lax.rem(slab + q, ns)}

    def giver(q):
        return {"dp": (xlo * nz + lax.rem(z + nz - q, nz)) * 2 + core, "slab": z}

    loads = [
        pltpu.make_async_copy(pre_hbm.at[0], pre_v, load_sem.at[0]),
        pltpu.make_async_copy(gn_hbm.at[0], gn_v, load_sem.at[1]),
    ]
    for c in loads:
        c.start()

    barrier = pltpu.get_barrier_semaphore()
    for q in range(1, ns):
        pl.semaphore_signal(barrier, inc=1, device_id=image_device(peer(q)), device_id_type=MESH)
    pl.semaphore_signal(barrier, inc=1, device_id=other_core, device_id_type=MESH)
    pl.semaphore_signal(barrier, inc=1, device_id=other_x, device_id_type=MESH)
    for q in range(1, ns):
        pl.semaphore_signal(barrier, inc=1, device_id=owner(q), device_id_type=MESH)
        pl.semaphore_signal(barrier, inc=1, device_id=giver(q), device_id_type=MESH)

    @pl.when(jnp.logical_not(own_final))
    def _():
        pl.semaphore_signal(barrier, inc=1, device_id=owner(0), device_id_type=MESH)
        pl.semaphore_signal(barrier, inc=1, device_id=giver(0), device_id_type=MESH)

    half = lax.div(slab, ns // 2)
    part = lax.rem(slab + ns // 2, ns)
    row_tap = 2 * half
    weights = [
        pltpu.make_async_copy(w_hbm.at[1], wv.at[0], w_sem.at[0]),
        pltpu.make_async_copy(w_hbm.at[row_tap], wv.at[1], w_sem.at[1]),
    ]

    def lanes(a, s):
        return pl.ds(pl.multiple_of(a * (cin // 2) + s * gran, gran), gran)

    own_x = [
        pltpu.make_async_copy(
            x_hbm.at[0, :, :, lanes(a, slab)],
            xr.at[slab, :, :, pl.ds(a * gran, gran)],
            x_loc.at[a],
        )
        for a in range(2)
    ]
    for c in own_x:
        c.start()

    for c in loads:
        c.wait()
    saved = pre_v[...].astype(F32)
    up = gn_v[...].astype(F32)

    def total(v):
        return jnp.sum(jnp.sum(v, axis=0), axis=0, keepdims=True)

    s1 = total(saved)
    centred = saved - s1 / (rows * cols)
    own_stats = [s1, total(centred * centred), total(up), total(up * centred)]
    st[slab] = jnp.concatenate(own_stats + [jnp.zeros((4, cout), F32)], axis=0)
    xf[:, side * 2 :, :] = jnp.zeros((ns * rows, pad - 2 * side, 2 * gran), BF16)
    gf[:, side * 2 :, :] = jnp.zeros((ns * rows, pad - 2 * side, cout), BF16)
    xc[...] = jnp.zeros(xc.shape, BF16)
    gc[...] = jnp.zeros(gc.shape, BF16)

    pl.semaphore_wait(barrier, (ns - 1) + 2 + 2 * ns - 2 * own_final.astype(jnp.int32))

    sends = []

    def send(src, dst, s_sem, r_sem, device):
        c = pltpu.make_async_remote_copy(
            src_ref=src, dst_ref=dst, send_sem=s_sem, recv_sem=r_sem,
            device_id=device, device_id_type=MESH,
        )
        c.start()
        sends.append(c)
        return c

    st_copies = [
        send(st.at[slab], st.at[slab], st_s.at[q], st_r.at[q], image_device(peer(q)))
        for q in range(1, ns)
    ]
    x_copies = {}
    for q in range(1, ns):
        for a in range(2):
            x_copies[q, a] = send(
                x_hbm.at[0, :, :, lanes(a, peer(q))],
                xr.at[slab, :, :, pl.ds(a * gran, gran)],
                x_s.at[q, a], x_r.at[q, a], image_device(peer(q)),
            )
    for c in weights:
        c.start()

    for c in st_copies:
        c.wait_recv()
    every = st[...]
    mean = jnp.sum(every[:, 0:1], axis=0) / cells
    m2 = jnp.zeros((1, cout), F32)
    sum_g = jnp.zeros((1, cout), F32)
    sum_gc = jnp.zeros((1, cout), F32)
    for k in range(ns):
        off = every[k, 0:1] / (rows * cols) - mean
        m2 = m2 + every[k, 1:2] + (rows * cols) * off * off
        sum_g = sum_g + every[k, 2:3]
        sum_gc = sum_gc + every[k, 3:4] + every[k, 2:3] * off
    inv_std = lax.rsqrt(m2 / cells + EPSILON)
    sum_gz = sum_gc * inv_std
    zhat = (saved - mean) * inv_std
    grad = (gain_ref[...] * inv_std) * (up - sum_g / cells - zhat * (sum_gz / cells))
    gr[slab] = grad.astype(BF16)
    g_copies = {
        q: send(gr.at[slab], gr.at[slab], g_s.at[q], g_r.at[q], image_device(peer(q)))
        for q in range(1, ns)
    }
    gb[...] = jnp.concatenate([sum_gz, sum_g, jnp.zeros((6, cout), F32)], axis=0)
    gbc_copy = send(gb, gbc, gc_s, gc_r, other_core)

    def unpack(block, full, corner, k):
        v = block[k]
        at = pl.ds(k * rows, rows)
        full[at, 0:cols, :] = v
        corner[at, 0:third, :] = v[:, cols - third :, :]

    unpack(gr, gf, gc, slab)
    for c in own_x:
        c.wait()
    unpack(xr, xf, xc, slab)

    gbc_copy.wait_recv()
    gbk[...] = gb[...] + gbc[...]
    gbx_copy = send(gbk, gbx, gl_s, gl_r, other_x)

    for q in range(1, ns):
        x_copies[q, 0].wait_recv()
        x_copies[q, 1].wait_recv()
        unpack(xr, xf, xc, source(q))
    for q in range(1, ns):
        g_copies[q].wait_recv()
        unpack(gr, gf, gc, source(q))

    gbx_copy.wait_recv()
    gbs[...] = gbk[...] + gbx[...]

    place = lax.rem(z + nz - slab, nz)

    def to_owners(src_of, dst, s_sem, r_sem, loc_sem):
        for q in range(1, ns):
            send(src_of(q), dst, s_sem.at[q], r_sem.at[place], owner(q))
        first = pltpu.make_async_remote_copy(
            src_ref=src_of(0), dst_ref=dst, send_sem=s_sem.at[0], recv_sem=r_sem.at[place],
            device_id=owner(0), device_id_type=MESH,
        )
        local = pltpu.make_async_copy(src_of(0), dst, loc_sem)

        @pl.when(own_final)
        def _():
            local.start()

        @pl.when(jnp.logical_not(own_final))
        def _():
            first.start()

        return first, local

    def from_givers(copies, dst, s_sem, r_sem):
        first, local = copies

        def arrival(idx):
            at = dst.at[lax.rem(z + idx, nz)]
            return pltpu.make_async_remote_copy(
                src_ref=at, dst_ref=at, send_sem=s_sem.at[0], recv_sem=r_sem.at[idx],
                device_id=other_core, device_id_type=MESH,
            )

        for idx in range(1, nz):
            arrival(idx).wait_recv()

        @pl.when(own_final)
        def _():
            local.wait()

        @pl.when(jnp.logical_not(own_final))
        def _():
            first.wait_send()
            arrival(0).wait_recv()

    gbf_copies = to_owners(lambda q: gbs, gbf.at[z], gf_s, gf_r, gb_loc)

    hh = ns * rows // 2

    def weight_tap(t):
        i, j = TAPS[t]
        h0, h1 = ((0, hh), (0, 2 * hh), (hh, 2 * hh))[i]
        g0, g1 = ((hh, 2 * hh), (0, 2 * hh), (0, hh))[i]
        xs = (xf[h0:h1, 0:side], xf[h0:h1], xc[h0:h1])[j]
        gs = (gc[g0:g1], gf[g0:g1], gf[g0:g1, 0:side])[j]
        n = xs.shape[0] * xs.shape[1]
        prod = lax.dot_general(
            xs.reshape(n, 2 * gran), gs.reshape(n, cout),
            (((0,), (0,)), ((), ())), preferred_element_type=F32,
        )
        dw[t] = prod.reshape(2, 2, gran // 2, cout)
        return send(
            dw.at[t, :, 1 - core], crecv.at[t], c_s.at[t], c_r.at[t], other_core
        )

    def core_stage(t, copy):
        copy.wait_recv()
        keep[t] = dw[t, xlo, core] + crecv[t, xlo]
        xsend[t] = (dw[t, 1 - xlo, core] + crecv[t, 1 - xlo]).astype(BF16)
        return send(xsend.at[t], xrecv.at[t], l_s.at[t], l_r.at[t], other_x)

    def x_stage(t, copy):
        copy.wait_recv()
        v = (keep[t] + xrecv[t].astype(F32)).reshape(ns, 8, cout)
        v = jnp.concatenate([v[:, :, : cout // 2], v[:, :, cout // 2 :]], axis=1)
        fsend[:, t] = v.astype(BF16)

    chunk = 256 if cin % 256 == 0 else cin

    def input_chunk(n, carry):
        at = pl.ds(pl.multiple_of(n * chunk, chunk), chunk)

        def prod(g, w):
            m = g.shape[0] * g.shape[1]
            return lax.dot_general(
                g.reshape(m, cout), w, (((1,), (1,)), ((), ())), preferred_element_type=F32
            ).reshape(g.shape[0], g.shape[1], chunk)

        mine, theirs = pl.ds(slab * rows, rows), pl.ds(part * rows, rows)
        mid = prod(gf[mine], wv[0, 1, at]) + prod(gf[theirs], wv[1, 1, at])
        first = prod(gc[mine], wv[0, 0, at]) + prod(gc[theirs], wv[1, 0, at])
        last = prod(gf[mine, 0:side], wv[0, 2, at]) + prod(gf[theirs, 0:side], wv[1, 2, at])
        tail = cols - third
        gin_v[:, :, at] = jnp.concatenate(
            [
                mid[:, :side] + first,
                mid[:, side:tail],
                mid[:, tail:cols] + last[:, :third],
            ],
            axis=1,
        ).astype(BF16)
        return carry

    nt = len(TAPS)
    c_copies, l_copies = {}, {}
    for step in range(nt + 1):
        if step < nt:
            c_copies[step] = weight_tap(step)
        if step >= 1:
            l_copies[step - 1] = core_stage(step - 1, c_copies[step - 1])
    for t in range(nt):
        x_stage(t, l_copies[t])
    f_copies = to_owners(
        lambda q: fsend.at[lax.rem(slab + q, ns)], frecv.at[z], f_s, f_r, f_loc
    )
    for c in weights:
        c.wait()
    lax.fori_loop(0, cin // chunk, input_chunk, 0)
    gin_copy = pltpu.make_async_copy(gin_v, gin_ref.at[0], gin_sem)
    gin_copy.start()

    from_givers(gbf_copies, gbf, gf_s, gf_r)
    both = jnp.sum(gbf[...], axis=0)
    gg_ref[...] = both[0:1]
    bg_ref[...] = both[1:2]
    from_givers(f_copies, frecv, f_s, f_r)
    acc = frecv[0].astype(F32)
    for k in range(1, nz):
        acc = acc + frecv[k].astype(F32)
    for t, (i, j) in enumerate(TAPS):
        wg_ref[i, j] = jnp.concatenate([acc[t, :8], acc[t, 8:]], axis=1)
    for c in sends:
        c.wait_send()
    gin_copy.wait()


def per_device(inputs, weight, pre_norm, grad_norm, norm_gain):
    ns = lax.axis_size("slab")
    nz = lax.axis_size("dp") // 4
    _, rows, cols, cin = inputs.shape
    cout = pre_norm.shape[3]
    sizes = (ns, nz, rows, cols, cin, cout)
    block = 2 * (cin // (2 * ns))
    height = ns * rows
    pad, side = 48, 16
    nt = len(TAPS)
    dma = pltpu.SemaphoreType.DMA
    any_spec = pl.BlockSpec(memory_space=pl.ANY)
    vmem_spec = pl.BlockSpec(memory_space=pltpu.VMEM)
    scratch = [
        pltpu.VMEM((rows, cols, cout), BF16),
        pltpu.VMEM((rows, cols, cout), BF16),
        pltpu.VMEM((ns, 8, cout), F32),
        pltpu.VMEM((ns, rows, cols, block), BF16),
        pltpu.VMEM((ns, rows, cols, cout), BF16),
        pltpu.VMEM((height, pad, block), BF16),
        pltpu.VMEM((height, side, block), BF16),
        pltpu.VMEM((height, pad, cout), BF16),
        pltpu.VMEM((height, side, cout), BF16),
        pltpu.VMEM((2, 3, cin, cout), BF16),
        pltpu.VMEM((rows, cols, cin), BF16),
        pltpu.VMEM((nt, 2, 2, block // 4, cout), F32),
        pltpu.VMEM((nt, 2, block // 4, cout), F32),
        pltpu.VMEM((nt, block // 4, cout), F32),
        pltpu.VMEM((nt, block // 4, cout), BF16),
        pltpu.VMEM((nt, block // 4, cout), BF16),
        pltpu.VMEM((ns, nt, 16, cout // 2), BF16),
        pltpu.VMEM((nz, nt, 16, cout // 2), BF16),
        pltpu.VMEM((8, cout), F32),
        pltpu.VMEM((8, cout), F32),
        pltpu.VMEM((8, cout), F32),
        pltpu.VMEM((8, cout), F32),
        pltpu.VMEM((8, cout), F32),
        pltpu.VMEM((nz, 8, cout), F32),
        dma((2,)), dma((2,)), dma((2,)), dma, dma, dma,
        dma((ns,)), dma((ns,)), dma((ns, 2)), dma((ns, 2)), dma((ns,)), dma((ns,)),
        dma((nt,)), dma((nt,)), dma((nt,)), dma((nt,)), dma((ns,)), dma((ns,)),
        dma, dma, dma, dma, dma((ns,)), dma((ns,)),
    ]
    gin, wg, gg, bg = pl.pallas_call(
        functools.partial(kernel, sizes),
        out_shape=(
            jax.ShapeDtypeStruct(inputs.shape, BF16),
            jax.ShapeDtypeStruct((3, 3, cin // (ns * nz * 4), cout), F32),
            jax.ShapeDtypeStruct((1, cout), F32),
            jax.ShapeDtypeStruct((1, cout), F32),
        ),
        in_specs=[any_spec, any_spec, any_spec, any_spec, vmem_spec],
        out_specs=(any_spec, vmem_spec, vmem_spec, vmem_spec),
        scratch_shapes=scratch,
        compiler_params=pltpu.CompilerParams(
            collective_id=0, has_side_effects=True, vmem_limit_bytes=56 * 1024 * 1024
        ),
    )(inputs, weight, pre_norm, grad_norm, norm_gain.reshape(1, cout))
    return gin, wg, gg.reshape(cout), bg.reshape(cout)


def solution(mesh):
    placed = (
        P("dp", "slab", None, None),
        P(),
        P("dp", "slab", None, None),
        P("dp", "slab", None, None),
        P(),
    )
    return jax.shard_map(
        per_device,
        mesh=mesh,
        in_specs=placed,
        out_specs=(P("dp", "slab", None, None), P(None, None, ("dp", "slab"), None), P(), P()),
        check_vma=False,
    )
```

time: 1450 us -> 85.1 us (0.06)
  the two profiles are of different devices: /device:TPU:130 before, /device:TPU:30 now
where the time goes in v1:
time: 85.1 us; the launch traced here: 84.9 us
  Pallas kernels  78 us (92%)
  local copies, waits for them, and re-layouts  6.21 us (7%)
    pallas_call x1, Pallas kernels, per_device(): pl.pallas_call(functools.partial(kernel, sizes), out_shape=(jax.ShapeDtyp...  78 us
    unnamed x4, local copies, waits for them, and re-layouts  6.21 us

profile of v1, /device:TPU:30, one launch (start us, length us, event | category | flops | bytes accessed | tf_op | source)
XLA Modules:
  0.0 84.9 jit_solution(9579881827987449096)
XLA Ops:
  0.6 78.0 %shard_map.84 = (bf16[1,6,36,2048]{3,2,1,0:T(8,128)(2,1)}, f32[3,3,8,256]{3,2,1,0:T(8,128)}, f32[1,256]{1,0:T(1,128)}, f32[1,256]{1,0:T(1,128)}) custom-call(bf16[1,6,36,2048]{3,2,1,0:T(8,128)(2,1)} %x_hbm.1, bf16[3,3,2048,256]{3,2,1,0:T(8,128)(2,1)} %w_hbm.1, bf16[1,6,36,256]{3,2,1,0:T(8,128)(2,1)} %pre_hbm.1, bf16[1,6,36,256]{3,2,1,0:T(8,128)(2,1)} %gn_hbm.1, ...), custom_call_target="tpu_custom_call" | custom-call | tf_op jit(solution)/shard_map/pallas_call | solution.py:373
  78.7 2.2 %copy.13 = bf16[1,6,36,2048]{3,2,1,0:T(8,128)(2,1)} copy(bf16[1,6,36,2048]{3,2,1,0:T(8,128)(2,1)} %get-tuple-element.16) | data formatting | bytes 1769472
  80.9 1.5 %copy.14 = f32[3,3,8,256]{3,2,1,0:T(8,128)} copy(f32[3,3,8,256]{3,2,1,0:T(8,128)} %get-tuple-element.17) | data formatting | bytes 147456
  82.4 1.2 %copy.15 = f32[256]{0:T(256)} copy(f32[256]{0:T(256)} %bitcast.5) | data formatting | bytes 2048
  83.6 1.2 %copy.16 = f32[256]{0:T(256)} copy(f32[256]{0:T(256)} %bitcast.4) | data formatting | bytes 2048

commit v2 on v1

v2 whole, which is shorter than its diff:
```python
import functools

import jax
import jax.numpy as jnp
from jax import lax
from jax.experimental import pallas as pl
from jax.experimental.pallas import tpu as pltpu
from jax.sharding import PartitionSpec as P

MESH = pl.DeviceIdType.MESH
F32 = jnp.float32
BF16 = jnp.bfloat16
EPSILON = 1e-05
TAPS = ((1, 1), (0, 1), (2, 1), (1, 0), (1, 2), (0, 0), (0, 2), (2, 0), (2, 2))
GROUPS = ((0, 1, 2), (3, 4, 5), (6, 7, 8))


def kernel(
    sizes,
    x_hbm, w_hbm, pre_hbm, gn_hbm, gain_ref,
    gin_ref, small_ref,
    pre_v, gn_v, st, xr, gr, xf, xc, gf, gc, wv, gin_v,
    dw, crecv, ssend, srecv, zsend, zrecv,
    gb, gbc, gbk, gbx, gbz,
    load_sem, w_sem, x_loc, gin_sem,
    st_s, st_r, x_s, x_r, g_s, g_r, c_s, c_r, s_s, s_r, z_s, z_r,
    gc_s, gc_r, gl_s, gl_r, gz_s, gz_r,
):
    ns, nz, rows, cols, cin, cout = sizes
    gran = cin // (2 * ns)
    pad = xf.shape[1]
    side = xc.shape[1]
    third = cols // 3
    cells = rows * cols * ns
    slab = lax.axis_index("slab")
    dp = lax.axis_index("dp")
    core = lax.rem(dp, 2)
    z = lax.rem(lax.div(dp, 2), nz)
    xlo = lax.div(dp, 2 * nz)
    other_core = {"dp": dp + 1 - 2 * core, "slab": slab}
    other_x = {"dp": dp + (1 - 2 * xlo) * (2 * nz), "slab": slab}
    nt = len(TAPS)

    def peer(q):
        return lax.rem(slab + q, ns)

    def source(q):
        return lax.rem(slab + ns - q, ns)

    def image_device(q):
        return {"dp": dp, "slab": peer(q)}

    def z_peer(q):
        return lax.rem(z + q, nz)

    def z_device(q):
        return {"dp": (xlo * nz + z_peer(q)) * 2 + core, "slab": slab}

    def pair_device(e, q):
        return {"dp": (xlo + e * (1 - 2 * xlo)) * (2 * nz) + lax.rem(dp, 2 * nz), "slab": peer(q)}

    pair_steps = [(e, q) for e in range(2) for q in range(ns) if e or q]

    loads = [
        pltpu.make_async_copy(pre_hbm.at[0], pre_v, load_sem.at[0]),
        pltpu.make_async_copy(gn_hbm.at[0], gn_v, load_sem.at[1]),
    ]
    for c in loads:
        c.start()

    barrier = pltpu.get_barrier_semaphore()
    friends = [pair_device(e, q) for e, q in pair_steps] + [other_core]
    friends += [z_device(q) for q in range(1, nz)]
    for friend in friends:
        pl.semaphore_signal(barrier, inc=1, device_id=friend, device_id_type=MESH)

    half = lax.div(slab, ns // 2)
    part = lax.rem(slab + ns // 2, ns)
    row_tap = 2 * half
    weights = [
        pltpu.make_async_copy(w_hbm.at[1], wv.at[0], w_sem.at[0]),
        pltpu.make_async_copy(w_hbm.at[row_tap], wv.at[1], w_sem.at[1]),
    ]

    def lanes(a, s):
        return pl.ds(pl.multiple_of(a * (cin // 2) + s * gran, gran), gran)

    own_x = [
        pltpu.make_async_copy(
            x_hbm.at[0, :, :, lanes(a, slab)],
            xr.at[slab, :, :, pl.ds(a * gran, gran)],
            x_loc.at[a],
        )
        for a in range(2)
    ]
    for c in own_x:
        c.start()

    for c in loads:
        c.wait()
    saved = pre_v[...].astype(F32)
    up = gn_v[...].astype(F32)

    def total(v):
        return jnp.sum(jnp.sum(v, axis=0), axis=0, keepdims=True)

    s1 = total(saved)
    centred = saved - s1 / (rows * cols)
    own_stats = [s1, total(centred * centred), total(up), total(up * centred)]
    st[slab] = jnp.concatenate(own_stats + [jnp.zeros((4, cout), F32)], axis=0)
    xf[:, side * 2 :, :] = jnp.zeros((ns * rows, pad - 2 * side, 2 * gran), BF16)
    gf[:, side * 2 :, :] = jnp.zeros((ns * rows, pad - 2 * side, cout), BF16)
    xc[...] = jnp.zeros(xc.shape, BF16)
    gc[...] = jnp.zeros(gc.shape, BF16)

    pl.semaphore_wait(barrier, len(friends))

    sends = []

    def send(src, dst, s_sem, r_sem, device):
        c = pltpu.make_async_remote_copy(
            src_ref=src, dst_ref=dst, send_sem=s_sem, recv_sem=r_sem,
            device_id=device, device_id_type=MESH,
        )
        c.start()
        sends.append(c)
        return c

    st_copies = [
        send(st.at[slab], st.at[slab], st_s.at[q], st_r.at[q], image_device(q))
        for q in range(1, ns)
    ]
    x_copies = {}
    for q in range(1, ns):
        for a in range(2):
            x_copies[q, a] = send(
                x_hbm.at[0, :, :, lanes(a, peer(q))],
                xr.at[slab, :, :, pl.ds(a * gran, gran)],
                x_s.at[q, a], x_r.at[q, a], image_device(q),
            )
    for c in weights:
        c.start()

    for c in st_copies:
        c.wait_recv()
    every = st[...]
    mean = jnp.sum(every[:, 0:1], axis=0) / cells
    m2 = jnp.zeros((1, cout), F32)
    sum_g = jnp.zeros((1, cout), F32)
    sum_gc = jnp.zeros((1, cout), F32)
    for k in range(ns):
        off = every[k, 0:1] / (rows * cols) - mean
        m2 = m2 + every[k, 1:2] + (rows * cols) * off * off
        sum_g = sum_g + every[k, 2:3]
        sum_gc = sum_gc + every[k, 3:4] + every[k, 2:3] * off
    inv_std = lax.rsqrt(m2 / cells + EPSILON)
    sum_gz = sum_gc * inv_std
    zhat = (saved - mean) * inv_std
    grad = (gain_ref[...] * inv_std) * (up - sum_g / cells - zhat * (sum_gz / cells))
    gr[slab] = grad.astype(BF16)
    g_order = [ns // 2] + [q for q in range(1, ns) if q != ns // 2]
    g_copies = {
        q: send(gr.at[slab], gr.at[slab], g_s.at[q], g_r.at[q], image_device(q)) for q in g_order
    }
    gb[...] = jnp.concatenate([sum_gz, sum_g, jnp.zeros((6, cout), F32)], axis=0)
    gbc_copy = send(gb, gbc, gc_s, gc_r, other_core)

    def unpack(block, full, corner, k):
        v = block[k]
        at = pl.ds(k * rows, rows)
        full[at, 0:cols, :] = v
        corner[at, 0:third, :] = v[:, cols - third :, :]

    unpack(gr, gf, gc, slab)
    for c in own_x:
        c.wait()
    unpack(xr, xf, xc, slab)

    gbc_copy.wait_recv()
    gbk[...] = gb[...] + gbc[...]
    gbx_copy = send(gbk, gbx, gl_s, gl_r, other_x)

    for q in range(1, ns):
        x_copies[q, 0].wait_recv()
        x_copies[q, 1].wait_recv()
        unpack(xr, xf, xc, source(q))
    gbx_copy.wait_recv()
    gbz[z] = gbk[...] + gbx[...]
    gbz_copies = [
        send(gbz.at[z], gbz.at[z], gz_s.at[q], gz_r.at[q], z_device(q)) for q in range(1, nz)
    ]

    hh = ns * rows // 2

    def weight_tap(t):
        i, j = TAPS[t]
        h0, h1 = ((0, hh), (0, 2 * hh), (hh, 2 * hh))[i]
        g0, g1 = ((hh, 2 * hh), (0, 2 * hh), (0, hh))[i]
        xs = (xf[h0:h1, 0:side], xf[h0:h1], xc[h0:h1])[j]
        gs = (gc[g0:g1], gf[g0:g1], gf[g0:g1, 0:side])[j]
        n = xs.shape[0] * xs.shape[1]
        prod = lax.dot_general(
            xs.reshape(n, 2 * gran), gs.reshape(n, cout),
            (((0,), (0,)), ((), ())), preferred_element_type=F32,
        )
        dw[t] = prod.reshape(2, 2, gran // 2, cout)
        return send(
            dw.at[t, :, 1 - core], crecv.at[t], c_s.at[t], c_r.at[t], other_core
        )

    def core_stage(t, copy):
        copy.wait_recv()
        v = (dw[t, :, core] + crecv[t]).reshape(2, ns, 8, cout)
        v = jnp.concatenate([v[:, :, :, : cout // 2], v[:, :, :, cout // 2 :]], axis=2)
        ssend[:, :, t] = v.astype(BF16)

    def pair_send(g):
        at = pl.ds(GROUPS[g][0], len(GROUPS[g]))
        copies = []
        for e, q in pair_steps:
            to_x = xlo + e * (1 - 2 * xlo)
            copies.append(
                send(
                    ssend.at[to_x, peer(q), at], srecv.at[xlo, slab, at],
                    s_s.at[g, e, q], s_r.at[g, e, q], pair_device(e, q),
                )
            )
        srecv[xlo, slab, at] = ssend[xlo, slab, at]
        return copies

    def z_send(g, copies):
        for c in copies:
            c.wait_recv()
        at = pl.ds(GROUPS[g][0], len(GROUPS[g]))
        zsend[:, at] = (srecv[0, :, at].astype(F32) + srecv[1, :, at].astype(F32)).astype(BF16)
        out = [
            send(zsend.at[z_peer(q), at], zrecv.at[z, at], z_s.at[g, q], z_r.at[g, q], z_device(q))
            for q in range(1, nz)
        ]
        zrecv[z, at] = zsend[z, at]
        return out

    chunk = 256 if cin % 256 == 0 else cin

    def input_chunk(n, carry):
        at = pl.ds(pl.multiple_of(n * chunk, chunk), chunk)

        def prod(g, w):
            m = g.shape[0] * g.shape[1]
            return lax.dot_general(
                g.reshape(m, cout), w, (((1,), (1,)), ((), ())), preferred_element_type=F32
            ).reshape(g.shape[0], g.shape[1], chunk)

        mine, theirs = pl.ds(slab * rows, rows), pl.ds(part * rows, rows)
        mid = prod(gf[mine], wv[0, 1, at]) + prod(gf[theirs], wv[1, 1, at])
        first = prod(gc[mine], wv[0, 0, at]) + prod(gc[theirs], wv[1, 0, at])
        last = prod(gf[mine, 0:side], wv[0, 2, at]) + prod(gf[theirs, 0:side], wv[1, 2, at])
        tail = cols - third
        gin_v[:, :, at] = jnp.concatenate(
            [
                mid[:, :side] + first,
                mid[:, side:tail],
                mid[:, tail:cols] + last[:, :third],
            ],
            axis=1,
        ).astype(BF16)
        return carry

    for q in g_order[:1]:
        g_copies[q].wait_recv()
        unpack(gr, gf, gc, source(q))
    for c in weights:
        c.wait()
    lax.fori_loop(0, cin // chunk, input_chunk, 0)
    gin_copy = pltpu.make_async_copy(gin_v, gin_ref.at[0], gin_sem)
    gin_copy.start()
    for q in g_order[1:]:
        g_copies[q].wait_recv()
        unpack(gr, gf, gc, source(q))

    ng = len(GROUPS)
    c_copies, s_copies, z_copies = {}, {}, {}
    for step in range(ng + 2):
        if step < ng:
            for t in GROUPS[step]:
                c_copies[t] = weight_tap(t)
        if 1 <= step <= ng:
            for t in GROUPS[step - 1]:
                core_stage(t, c_copies[t])
            s_copies[step - 1] = pair_send(step - 1)
        if step >= 2:
            z_copies[step - 2] = z_send(step - 2, s_copies[step - 2])

    for c in gbz_copies:
        c.wait_recv()
    small_ref[nt] = jnp.sum(gbz[...], axis=0)
    for g in range(ng):
        for c in z_copies[g]:
            c.wait_recv()
        at = pl.ds(GROUPS[g][0], len(GROUPS[g]))
        acc = zrecv[0, at].astype(F32)
        for k in range(1, nz):
            acc = acc + zrecv[k, at].astype(F32)
        small_ref[at] = jnp.concatenate([acc[:, :8], acc[:, 8:]], axis=2)
    for c in sends:
        c.wait_send()
    gin_copy.wait()


def results(gin_in, small_in, gin_ref, wg_ref, gg_ref, bg_ref, sem):
    copy = pltpu.make_async_copy(gin_in, gin_ref, sem)
    copy.start()
    for t, (i, j) in enumerate(TAPS):
        wg_ref[i, j] = small_in[t]
    gg_ref[...] = small_in[len(TAPS), 0:1]
    bg_ref[...] = small_in[len(TAPS), 1:2]
    copy.wait()


def per_device(inputs, weight, pre_norm, grad_norm, norm_gain):
    ns = lax.axis_size("slab")
    nz = lax.axis_size("dp") // 4
    _, rows, cols, cin = inputs.shape
    cout = pre_norm.shape[3]
    sizes = (ns, nz, rows, cols, cin, cout)
    block = 2 * (cin // (2 * ns))
    height = ns * rows
    pad, side = 48, 16
    nt, ng = len(TAPS), len(GROUPS)
    dma = pltpu.SemaphoreType.DMA
    any_spec = pl.BlockSpec(memory_space=pl.ANY)
    vmem_spec = pl.BlockSpec(memory_space=pltpu.VMEM)
    scratch = [
        pltpu.VMEM((rows, cols, cout), BF16),
        pltpu.VMEM((rows, cols, cout), BF16),
        pltpu.VMEM((ns, 8, cout), F32),
        pltpu.VMEM((ns, rows, cols, block), BF16),
        pltpu.VMEM((ns, rows, cols, cout), BF16),
        pltpu.VMEM((height, pad, block), BF16),
        pltpu.VMEM((height, side, block), BF16),
        pltpu.VMEM((height, pad, cout), BF16),
        pltpu.VMEM((height, side, cout), BF16),
        pltpu.VMEM((2, 3, cin, cout), BF16),
        pltpu.VMEM((rows, cols, cin), BF16),
        pltpu.VMEM((nt, 2, 2, block // 4, cout), F32),
        pltpu.VMEM((nt, 2, block // 4, cout), F32),
        pltpu.VMEM((2, ns, nt, 16, cout // 2), BF16),
        pltpu.VMEM((2, ns, nt, 16, cout // 2), BF16),
        pltpu.VMEM((nz, nt, 16, cout // 2), BF16),
        pltpu.VMEM((nz, nt, 16, cout // 2), BF16),
        pltpu.VMEM((8, cout), F32),
        pltpu.VMEM((8, cout), F32),
        pltpu.VMEM((8, cout), F32),
        pltpu.VMEM((8, cout), F32),
        pltpu.VMEM((nz, 8, cout), F32),
        dma((2,)), dma((2,)), dma((2,)), dma,
        dma((ns,)), dma((ns,)), dma((ns, 2)), dma((ns, 2)), dma((ns,)), dma((ns,)),
        dma((nt,)), dma((nt,)), dma((ng, 2, ns)), dma((ng, 2, ns)), dma((ng, nz)), dma((ng, nz)),
        dma, dma, dma, dma, dma((nz,)), dma((nz,)),
    ]
    gin, small = pl.pallas_call(
        functools.partial(kernel, sizes),
        out_shape=(
            jax.ShapeDtypeStruct(inputs.shape, BF16),
            jax.ShapeDtypeStruct((nt + 1, 8, cout), F32),
        ),
        in_specs=[any_spec, any_spec, any_spec, any_spec, vmem_spec],
        out_specs=(any_spec, vmem_spec),
        scratch_shapes=scratch,
        compiler_params=pltpu.CompilerParams(
            collective_id=0, has_side_effects=True, vmem_limit_bytes=56 * 1024 * 1024
        ),
    )(inputs, weight, pre_norm, grad_norm, norm_gain.reshape(1, cout))
    gin, wg, gg, bg = pl.pallas_call(
        results,
        out_shape=(
            jax.ShapeDtypeStruct(inputs.shape, BF16),
            jax.ShapeDtypeStruct((3, 3, 8, cout), F32),
            jax.ShapeDtypeStruct((1, cout), F32),
            jax.ShapeDtypeStruct((1, cout), F32),
        ),
        in_specs=[any_spec, vmem_spec],
        out_specs=(any_spec, vmem_spec, vmem_spec, vmem_spec),
        scratch_shapes=[dma],
    )(gin, small)
    return gin, wg, gg.reshape(cout), bg.reshape(cout)


def solution(mesh):
    placed = (
        P("dp", "slab", None, None),
        P(),
        P("dp", "slab", None, None),
        P("dp", "slab", None, None),
        P(),
    )
    return jax.shard_map(
        per_device,
        mesh=mesh,
        in_specs=placed,
        out_specs=(P("dp", "slab", None, None), P(None, None, ("dp", "slab"), None), P(), P()),
        check_vma=False,
    )
```

time: 85.1 us -> 92 us (1.081)
  the two profiles are of different devices: /device:TPU:30 before, /device:TPU:8 now
where the time goes in v2:
time: 92 us; the launch traced here: 91.8 us
  Pallas kernels  91.2 us (99%)
    pallas_call x1, Pallas kernels, per_device(): pl.pallas_call(functools.partial(kernel, sizes), out_shape=(jax.ShapeDtyp...  58.8 us
    pallas_call x1, Pallas kernels, per_device(): pl.pallas_call(results, out_shape=(jax.ShapeDtypeStruct(inputs.shape, BF1...  32.4 us

profile of v2, /device:TPU:8, one launch (start us, length us, event | category | flops | bytes accessed | tf_op | source)
XLA Modules:
  0.0 91.8 jit_solution(2843041064270774142)
XLA Ops:
  0.6 58.8 %shard_map.84 = (bf16[1,6,36,2048]{3,2,1,0:T(8,128)(2,1)}, f32[10,8,256]{2,1,0:T(8,128)}) custom-call(bf16[1,6,36,2048]{3,2,1,0:T(8,128)(2,1)} %x_hbm.1, bf16[3,3,2048,256]{3,2,1,0:T(8,128)(2,1)} %w_hbm.1, bf16[1,6,36,256]{3,2,1,0:T(8,128)(2,1)} %pre_hbm.1, bf16[1,6,36,256]{3,2,1,0:T(8,128)(2,1)} %gn_hbm.1, f32[1,256]{1,0:T(1,128)} %bitcast.3), custom_call_target="tpu_custom_call" | custom-call | tf_op jit(solution)/shard_map/pallas_call | solution.py:361
  59.4 32.4 %shard_map.85 = (bf16[1,6,36,2048]{3,2,1,0:T(8,128)(2,1)}, f32[3,3,8,256]{3,2,1,0:T(8,128)}, f32[1,256]{1,0:T(1,128)}, f32[1,256]{1,0:T(1,128)}) custom-call(bf16[1,6,36,2048]{3,2,1,0:T(8,128)(2,1)} %get-tuple-element.10.gin_in, f32[10,8,256]{2,1,0:T(8,128)} %get-tuple-element.11.small_in), custom_call_target="tpu_custom_call" | custom-call | tf_op jit(solution)/shard_map/pallas_call | solution.py:374

commit v3 on v2

--- a/solution.py
+++ b/solution.py
@@ -307,14 +307,25 @@
     gin_copy.wait()
 
 
-def results(gin_in, small_in, gin_ref, wg_ref, gg_ref, bg_ref, sem):
-    copy = pltpu.make_async_copy(gin_in, gin_ref, sem)
-    copy.start()
+def results(gin_in, small_in, gin_ref, wg_ref, gg_ref, bg_ref, held, in_sem, out_sem):
+    rows = held.shape[0]
+    into = [
+        pltpu.make_async_copy(gin_in.at[0, r], held.at[r], in_sem.at[r]) for r in range(rows)
+    ]
+    out = [
+        pltpu.make_async_copy(held.at[r], gin_ref.at[0, r], out_sem.at[r]) for r in range(rows)
+    ]
+    for c in into:
+        c.start()
     for t, (i, j) in enumerate(TAPS):
         wg_ref[i, j] = small_in[t]
     gg_ref[...] = small_in[len(TAPS), 0:1]
     bg_ref[...] = small_in[len(TAPS), 1:2]
-    copy.wait()
+    for r in range(rows):
+        into[r].wait()
+        out[r].start()
+    for c in out:
+        c.wait()
 
 
 def per_device(inputs, weight, pre_norm, grad_norm, norm_gain):
@@ -381,7 +392,7 @@
         ),
         in_specs=[any_spec, vmem_spec],
         out_specs=(any_spec, vmem_spec, vmem_spec, vmem_spec),
-        scratch_shapes=[dma],
+        scratch_shapes=[pltpu.VMEM((rows, cols, cin), BF16), dma((rows,)), dma((rows,))],
     )(gin, small)
     return gin, wg, gg.reshape(cout), bg.reshape(cout)
 

time: 92 us -> 63.2 us (0.69)
  Pallas kernels: 91.2 us -> 62.4 us
    pallas_call x1, Pallas kernels: 32.4 us -> 3.59 us  [per_device(): pl.pallas_call(results, out_shape=(jax.ShapeDtypeStruct(inputs.shape, BF1...]
where the time goes in v3:
time: 63.2 us; the launch traced here: 63 us
  Pallas kernels  62.4 us (99%)
  between operations  0.64 us (1%)
    pallas_call x1, Pallas kernels, per_device(): pl.pallas_call(functools.partial(kernel, sizes), out_shape=(jax.ShapeDtyp...  58.8 us
    pallas_call x1, Pallas kernels, per_device(): pl.pallas_call(results, out_shape=(jax.ShapeDtypeStruct(inputs.shape, BF1...  3.59 us

profile of v3, /device:TPU:8, one launch (start us, length us, event | category | flops | bytes accessed | tf_op | source)
XLA Modules:
  0.0 63.0 jit_solution(10821257147203677823)
XLA Ops:
  0.6 58.8 %shard_map.84 = (bf16[1,6,36,2048]{3,2,1,0:T(8,128)(2,1)}, f32[10,8,256]{2,1,0:T(8,128)}) custom-call(bf16[1,6,36,2048]{3,2,1,0:T(8,128)(2,1)} %x_hbm.1, bf16[3,3,2048,256]{3,2,1,0:T(8,128)(2,1)} %w_hbm.1, bf16[1,6,36,256]{3,2,1,0:T(8,128)(2,1)} %pre_hbm.1, bf16[1,6,36,256]{3,2,1,0:T(8,128)(2,1)} %gn_hbm.1, f32[1,256]{1,0:T(1,128)} %bitcast.3), custom_call_target="tpu_custom_call" | custom-call | tf_op jit(solution)/shard_map/pallas_call | solution.py:372
  59.4 3.6 %shard_map.85 = (bf16[1,6,36,2048]{3,2,1,0:T(8,128)(2,1)}, f32[3,3,8,256]{3,2,1,0:T(8,128)}, f32[1,256]{1,0:T(1,128)}, f32[1,256]{1,0:T(1,128)}) custom-call(bf16[1,6,36,2048]{3,2,1,0:T(8,128)(2,1)} %get-tuple-element.10.gin_in, f32[10,8,256]{2,1,0:T(8,128)} %get-tuple-element.11.small_in), custom_call_target="tpu_custom_call" | custom-call | tf_op jit(solution)/shard_map/pallas_call | solution.py:385

commit v4 on v3

--- a/solution.py
+++ b/solution.py
@@ -17,9 +17,9 @@
 
 def kernel(
     sizes,
-    x_hbm, w_hbm, pre_hbm, gn_hbm, gain_ref,
-    gin_ref, small_ref,
-    pre_v, gn_v, st, xr, gr, xf, xc, gf, gc, wv, gin_v,
+    x_hbm, w_hbm, pre_hbm, gn_hbm, gain_hbm,
+    gin_ref, wg_ref, gg_ref, bg_ref,
+    pre_v, gn_v, gain_v, st, xr, gr, xf, xc, gf, gc, wv, gin_v,
     dw, crecv, ssend, srecv, zsend, zrecv,
     gb, gbc, gbk, gbx, gbz,
     load_sem, w_sem, x_loc, gin_sem,
@@ -64,12 +64,13 @@
     loads = [
         pltpu.make_async_copy(pre_hbm.at[0], pre_v, load_sem.at[0]),
         pltpu.make_async_copy(gn_hbm.at[0], gn_v, load_sem.at[1]),
+        pltpu.make_async_copy(gain_hbm, gain_v, load_sem.at[2]),
     ]
     for c in loads:
         c.start()
 
     barrier = pltpu.get_barrier_semaphore()
-    friends = [pair_device(e, q) for e, q in pair_steps] + [other_core]
+    friends = [image_device(q) for q in range(1, ns)] + [other_core, other_x]
     friends += [z_device(q) for q in range(1, nz)]
     for friend in friends:
         pl.semaphore_signal(barrier, inc=1, device_id=friend, device_id_type=MESH)
@@ -93,8 +94,6 @@
         )
         for a in range(2)
     ]
-    for c in own_x:
-        c.start()
 
     for c in loads:
         c.wait()
@@ -108,11 +107,6 @@
     centred = saved - s1 / (rows * cols)
     own_stats = [s1, total(centred * centred), total(up), total(up * centred)]
     st[slab] = jnp.concatenate(own_stats + [jnp.zeros((4, cout), F32)], axis=0)
-    xf[:, side * 2 :, :] = jnp.zeros((ns * rows, pad - 2 * side, 2 * gran), BF16)
-    gf[:, side * 2 :, :] = jnp.zeros((ns * rows, pad - 2 * side, cout), BF16)
-    xc[...] = jnp.zeros(xc.shape, BF16)
-    gc[...] = jnp.zeros(gc.shape, BF16)
-
     pl.semaphore_wait(barrier, len(friends))
 
     sends = []
@@ -138,8 +132,12 @@
                 xr.at[slab, :, :, pl.ds(a * gran, gran)],
                 x_s.at[q, a], x_r.at[q, a], image_device(q),
             )
-    for c in weights:
+    for c in own_x + weights:
         c.start()
+    xf[:, side * 2 :, :] = jnp.zeros((ns * rows, pad - 2 * side, 2 * gran), BF16)
+    gf[:, side * 2 :, :] = jnp.zeros((ns * rows, pad - 2 * side, cout), BF16)
+    xc[...] = jnp.zeros(xc.shape, BF16)
+    gc[...] = jnp.zeros(gc.shape, BF16)
 
     for c in st_copies:
         c.wait_recv()
@@ -156,7 +154,7 @@
     inv_std = lax.rsqrt(m2 / cells + EPSILON)
     sum_gz = sum_gc * inv_std
     zhat = (saved - mean) * inv_std
-    grad = (gain_ref[...] * inv_std) * (up - sum_g / cells - zhat * (sum_gz / cells))
+    grad = (gain_v[...] * inv_std) * (up - sum_g / cells - zhat * (sum_gz / cells))
     gr[slab] = grad.astype(BF16)
     g_order = [ns // 2] + [q for q in range(1, ns) if q != ns // 2]
     g_copies = {
@@ -266,15 +264,7 @@
         ).astype(BF16)
         return carry
 
-    for q in g_order[:1]:
-        g_copies[q].wait_recv()
-        unpack(gr, gf, gc, source(q))
-    for c in weights:
-        c.wait()
-    lax.fori_loop(0, cin // chunk, input_chunk, 0)
-    gin_copy = pltpu.make_async_copy(gin_v, gin_ref.at[0], gin_sem)
-    gin_copy.start()
-    for q in g_order[1:]:
+    for q in g_order:
         g_copies[q].wait_recv()
         unpack(gr, gf, gc, source(q))
 
@@ -288,12 +278,23 @@
             for t in GROUPS[step - 1]:
                 core_stage(t, c_copies[t])
             s_copies[step - 1] = pair_send(step - 1)
+        if step == 2:
+            for c in weights:
+                c.wait()
+        if step >= 2:
+            done = (step - 2) * (cin // chunk) // ng
+            lax.fori_loop(done, (step - 1) * (cin // chunk) // ng, input_chunk, 0)
+        if step == ng + 1:
+            gin_copy = pltpu.make_async_copy(gin_v, gin_ref.at[0], gin_sem)
+            gin_copy.start()
         if step >= 2:
             z_copies[step - 2] = z_send(step - 2, s_copies[step - 2])
 
     for c in gbz_copies:
         c.wait_recv()
-    small_ref[nt] = jnp.sum(gbz[...], axis=0)
+    both = jnp.sum(gbz[...], axis=0)
+    gg_ref[...] = both[0:1]
+    bg_ref[...] = both[1:2]
     for g in range(ng):
         for c in z_copies[g]:
             c.wait_recv()
@@ -301,13 +302,15 @@
         acc = zrecv[0, at].astype(F32)
         for k in range(1, nz):
             acc = acc + zrecv[k, at].astype(F32)
-        small_ref[at] = jnp.concatenate([acc[:, :8], acc[:, 8:]], axis=2)
+        acc = jnp.concatenate([acc[:, :8], acc[:, 8:]], axis=2)
+        for n, t in enumerate(GROUPS[g]):
+            wg_ref[TAPS[t]] = acc[n]
     for c in sends:
         c.wait_send()
     gin_copy.wait()
 
 
-def results(gin_in, small_in, gin_ref, wg_ref, gg_ref, bg_ref, held, in_sem, out_sem):
+def results(gin_in, wg_in, gg_in, bg_in, gin_ref, wg_ref, gg_ref, bg_ref, held, in_sem, out_sem, sem):
     rows = held.shape[0]
     into = [
         pltpu.make_async_copy(gin_in.at[0, r], held.at[r], in_sem.at[r]) for r in range(rows)
@@ -315,16 +318,18 @@
     out = [
         pltpu.make_async_copy(held.at[r], gin_ref.at[0, r], out_sem.at[r]) for r in range(rows)
     ]
-    for c in into:
+    small = [
+        pltpu.make_async_copy(wg_in.at[i], wg_ref.at[i], sem.at[i]) for i in range(3)
+    ] + [
+        pltpu.make_async_copy(gg_in, gg_ref, sem.at[3]),
+        pltpu.make_async_copy(bg_in, bg_ref, sem.at[4]),
+    ]
+    for c in into + small:
         c.start()
-    for t, (i, j) in enumerate(TAPS):
-        wg_ref[i, j] = small_in[t]
-    gg_ref[...] = small_in[len(TAPS), 0:1]
-    bg_ref[...] = small_in[len(TAPS), 1:2]
     for r in range(rows):
         into[r].wait()
         out[r].start()
-    for c in out:
+    for c in small + out:
         c.wait()
 
 
@@ -344,6 +349,7 @@
     scratch = [
         pltpu.VMEM((rows, cols, cout), BF16),
         pltpu.VMEM((rows, cols, cout), BF16),
+        pltpu.VMEM((1, cout), F32),
         pltpu.VMEM((ns, 8, cout), F32),
         pltpu.VMEM((ns, rows, cols, block), BF16),
         pltpu.VMEM((ns, rows, cols, cout), BF16),
@@ -364,19 +370,22 @@
         pltpu.VMEM((8, cout), F32),
         pltpu.VMEM((8, cout), F32),
         pltpu.VMEM((nz, 8, cout), F32),
-        dma((2,)), dma((2,)), dma((2,)), dma,
+        dma((3,)), dma((2,)), dma((2,)), dma,
         dma((ns,)), dma((ns,)), dma((ns, 2)), dma((ns, 2)), dma((ns,)), dma((ns,)),
         dma((nt,)), dma((nt,)), dma((ng, 2, ns)), dma((ng, 2, ns)), dma((ng, nz)), dma((ng, nz)),
         dma, dma, dma, dma, dma((nz,)), dma((nz,)),
     ]
-    gin, small = pl.pallas_call(
+    shapes = (
+        jax.ShapeDtypeStruct(inputs.shape, BF16),
+        jax.ShapeDtypeStruct((3, 3, 8, cout), F32),
+        jax.ShapeDtypeStruct((1, cout), F32),
+        jax.ShapeDtypeStruct((1, cout), F32),
+    )
+    staged = pl.pallas_call(
         functools.partial(kernel, sizes),
-        out_shape=(
-            jax.ShapeDtypeStruct(inputs.shape, BF16),
-            jax.ShapeDtypeStruct((nt + 1, 8, cout), F32),
-        ),
-        in_specs=[any_spec, any_spec, any_spec, any_spec, vmem_spec],
-        out_specs=(any_spec, vmem_spec),
+        out_shape=shapes,
+        in_specs=[any_spec] * 5,
+        out_specs=(any_spec, vmem_spec, vmem_spec, vmem_spec),
         scratch_shapes=scratch,
         compiler_params=pltpu.CompilerParams(
             collective_id=0, has_side_effects=True, vmem_limit_bytes=56 * 1024 * 1024
@@ -384,16 +393,13 @@
     )(inputs, weight, pre_norm, grad_norm, norm_gain.reshape(1, cout))
     gin, wg, gg, bg = pl.pallas_call(
         results,
-        out_shape=(
-            jax.ShapeDtypeStruct(inputs.shape, BF16),
-            jax.ShapeDtypeStruct((3, 3, 8, cout), F32),
-            jax.ShapeDtypeStruct((1, cout), F32),
-            jax.ShapeDtypeStruct((1, cout), F32),
-        ),
-        in_specs=[any_spec, vmem_spec],
-        out_specs=(any_spec, vmem_spec, vmem_spec, vmem_spec),
-        scratch_shapes=[pltpu.VMEM((rows, cols, cin), BF16), dma((rows,)), dma((rows,))],
-    )(gin, small)
+        out_shape=shapes,
+        in_specs=[any_spec] * 4,
+        out_specs=(any_spec,) * 4,
+        scratch_shapes=[
+            pltpu.VMEM((rows, cols, cin), BF16), dma((rows,)), dma((rows,)), dma((5,))
+        ],
+    )(*staged)
     return gin, wg, gg.reshape(cout), bg.reshape(cout)
 
 

time: 63.2 us -> 60.6 us (0.959)
  Pallas kernels: 62.4 us -> 59.2 us
    pallas_call x2, Pallas kernels: 62.4 us -> 59.2 us  [the longest x1 55.7 us: per_device(): pl.pallas_call(functools.partial(kernel, sizes), out_shape=shapes, in_spe...]
where the time goes in v4:
time: 60.6 us; the launch traced here: 59.9 us
  Pallas kernels  59.2 us (98%)
  between operations  0.64 us (1%)
    pallas_call x1, Pallas kernels, per_device(): pl.pallas_call(functools.partial(kernel, sizes), out_shape=shapes, in_spe...  55.7 us
    pallas_call x1, Pallas kernels, per_device(): pl.pallas_call(results, out_shape=shapes, in_specs=[any_spec] * 4, out_sp...  3.57 us

profile of v4, /device:TPU:8, one launch (start us, length us, event | category | flops | bytes accessed | tf_op | source)
XLA Modules:
  0.0 59.9 jit_solution(18026058578830755652)
XLA Ops:
  0.6 55.7 %shard_map.84 = (bf16[1,6,36,2048]{3,2,1,0:T(8,128)(2,1)}, f32[3,3,8,256]{3,2,1,0:T(8,128)}, f32[1,256]{1,0:T(1,128)}, f32[1,256]{1,0:T(1,128)}) custom-call(bf16[1,6,36,2048]{3,2,1,0:T(8,128)(2,1)} %x_hbm.1, bf16[3,3,2048,256]{3,2,1,0:T(8,128)(2,1)} %w_hbm.1, bf16[1,6,36,256]{3,2,1,0:T(8,128)(2,1)} %pre_hbm.1, bf16[1,6,36,256]{3,2,1,0:T(8,128)(2,1)} %gn_hbm.1, ...), custom_call_target="tpu_custom_call" | custom-call | tf_op jit(solution)/shard_map/pallas_call | solution.py:384
  56.3 3.6 %shard_map.85 = (bf16[1,6,36,2048]{3,2,1,0:T(8,128)(2,1)}, f32[3,3,8,256]{3,2,1,0:T(8,128)}, f32[1,256]{1,0:T(1,128)}, f32[1,256]{1,0:T(1,128)}) custom-call(bf16[1,6,36,2048]{3,2,1,0:T(8,128)(2,1)} %get-tuple-element.12.gin_in, f32[3,3,8,256]{3,2,1,0:T(8,128)} %get-tuple-element.13.wg_in, f32[1,256]{1,0:T(1,128)} %get-tuple-element.14.gg_in, ...), custom_call_target="tpu_custom_call" | custom-call | tf_op jit(solution)/shard_map/pallas_call | solution.py:394
